TPU v7x, 32 devices: a whole 2x2x4 slice. The times are simulated.
32 devices in a mesh: grp: 2 (over x), row: 16 (over z, y, core).
Axes of the slice: x: 2, y: 2, z: 4, core: 2. Of those that a mesh axis runs over, the one named last changes fastest.
Arguments:
- tokens: bfloat16 [512, 8192], P(('grp', 'row')), parts along dimension 0, may hold values from -6 to 6
- attention_norm_gain: float32 [8192], replicated, may hold values from 0.1 to 1.9
- query_weight: bfloat16 [8192, 8192], P(None, 'row'), may hold values from -0.0625 to 0.0625
- keyvalue_weight: bfloat16 [8192, 2, 1024], P(None, None, 'row'), may hold values from -0.0625 to 0.0625
- adapter_down_weight: bfloat16 [64, 64, 8192], P('row'), may hold values from -0.0625 to 0.0625
- adapter_query_up: bfloat16 [64, 32, 8192], P(None, None, 'row'), may hold values from -1 to 1
- adapter_value_up: bfloat16 [64, 32, 1024], P(None, None, 'row'), may hold values from -1 to 1
- cached_rotated_keys: bfloat16 [512, 48, 1024], P(('grp', 'row')), parts along dimension 0, may hold values from -102 to 102
- cached_value_rows: bfloat16 [512, 48, 1024], P(('grp', 'row')), parts along dimension 0, may hold values from -6 to 6
- row_adapter_index: int32 [512], P('grp'), parts along dimension 0, may hold values from 0 to 63, as said below
Outputs:
- context: bfloat16 [512, 8192], P(('grp', 'row')), parts along dimension 0
- new_keys: bfloat16 [512, 1024], P(('grp', 'row')), parts along dimension 0
- incoming_values: bfloat16 [512, 1024], P(('grp', 'row')), parts along dimension 0
There are 2 independent parts, one for each index of `grp`. A program takes and returns all parts, laid end to end along the dimension named above; an argument that names none is the same for every part. Nothing has to cross between parts.
Inputs may be any that keep to these rules, and one draw needn't show every extreme that they name: `row_adapter_index`: the adapter a is owned by index a // 4 of row; no index owns the adapters of more than 64 rows, and 16 / 8 indices (two here, eight on the larger slice) own exactly 64.
All inputs are finite; a program needn't handle non-finite values.
Results may differ from a plain program's by a relative error of at most 0.009.
The roundings to bfloat16 on the way count: a program that leaves them out, or rounds other values in their place, can miss the bound.
Values may be sent and summed in bfloat16 or wider, within the bound.
A program may use at most 128 MiB of HBM per device.

v0:
```python
import math

import jax
import jax.numpy as jnp
from jax import lax
from jax.sharding import PartitionSpec as P

HEAD_DIM = 128
CAPO = 64


eps_value = 1e-05
adapter_scale = 2.0
rope_base = 500000.0


def rms_normed(tokens, attention_norm_gain):
    values = tokens.astype(jnp.float32)
    mean_square = jnp.mean(values * values, axis=-1, keepdims=True)
    return (values * lax.rsqrt(mean_square + eps_value) * attention_norm_gain).astype(jnp.bfloat16)


def rotate(vectors, position):
    half_width = vectors.shape[-1] // 2
    fraction = jnp.arange(half_width, dtype=jnp.float32) / half_width
    angles = position * jnp.exp(-fraction * math.log(rope_base))
    cosine = jnp.cos(angles)
    sine_part = jnp.sin(angles)
    front_half = vectors[..., :half_width]
    back_half = vectors[..., half_width:]
    return jnp.concatenate(
        [front_half * cosine - back_half * sine_part, back_half * cosine + front_half * sine_part],
        axis=-1,
    )


def slot_table(row_adapter_index, per_adapter_rows, owners):
    row_total = row_adapter_index.shape[0]
    sorted_rows = jnp.argsort(row_adapter_index, stable=True)
    owner_of = row_adapter_index // per_adapter_rows
    counts = jnp.sum(
        (owner_of[:, None] == jnp.arange(owners, dtype=jnp.int32)[None, :]).astype(jnp.int32),
        axis=0,
    )
    offsets = jnp.cumsum(counts) - counts
    places = jnp.arange(CAPO, dtype=jnp.int32)
    positions = offsets[:, None] + places[None, :]
    filled = places[None, :] < counts[:, None]
    row_table = jnp.where(filled, sorted_rows[jnp.minimum(positions, row_total - 1)], 0)
    return (row_table, filled)


def attend(query, key_new, value_new, cached_rotated_keys, cached_value_rows):
    rows_here = query.shape[0]
    heads_here = query.shape[1] // HEAD_DIM
    kv_heads = key_new.shape[1] // HEAD_DIM
    prefix_len = cached_rotated_keys.shape[1]
    position = float(prefix_len)
    rot_query = rotate(
        query.astype(jnp.float32).reshape(rows_here, heads_here, HEAD_DIM), position
    ).astype(jnp.bfloat16)
    rot_key = rotate(
        key_new.astype(jnp.float32).reshape(rows_here, kv_heads, HEAD_DIM), position
    ).astype(jnp.bfloat16)
    grouped = rot_query.reshape(rows_here, kv_heads, heads_here // kv_heads, HEAD_DIM)
    past_keys = cached_rotated_keys.reshape(rows_here, prefix_len, kv_heads, HEAD_DIM)
    past_values = cached_value_rows.reshape(rows_here, prefix_len, kv_heads, HEAD_DIM)
    scale = HEAD_DIM ** (-0.5)
    old_scores = (
        jnp.einsum("rkgd,rpkd->rkgp", grouped, past_keys, preferred_element_type=jnp.float32)
        * scale
    )
    new_scores = (
        jnp.einsum("rkgd,rkd->rkg", grouped, rot_key, preferred_element_type=jnp.float32)[..., None]
        * scale
    )
    scores = jnp.concatenate([old_scores, new_scores], axis=-1)
    peak = jnp.max(scores, axis=-1, keepdims=True)
    expo = jnp.exp(scores - peak)
    weights = (expo / jnp.sum(expo, axis=-1, keepdims=True)).astype(jnp.bfloat16)
    mixed = jnp.einsum(
        "rkgp,rpkd->rkgd",
        weights[..., :prefix_len],
        past_values,
        preferred_element_type=jnp.float32,
    )
    fresh_values = value_new.reshape(rows_here, kv_heads, 1, HEAD_DIM).astype(jnp.float32)
    mixed = mixed + weights[..., prefix_len:].astype(jnp.float32) * fresh_values
    context = mixed.reshape(rows_here, heads_here * HEAD_DIM).astype(jnp.bfloat16)
    return (context, rot_key.reshape(rows_here, kv_heads * HEAD_DIM), value_new)


def shards(
    tokens,
    attention_norm_gain,
    query_weight,
    keyvalue_weight,
    adapter_down_weight,
    adapter_query_up,
    adapter_value_up,
    cached_rotated_keys,
    cached_value_rows,
    row_adapter_index,
):
    normed = rms_normed(tokens, attention_norm_gain)
    owner_index = lax.axis_index("row")
    owners = lax.axis_size("row")
    per_adapter_rows = adapter_down_weight.shape[0]
    reduced_rank_state = adapter_query_up.shape[1]
    row_total = row_adapter_index.shape[0]
    model_width = normed.shape[1]
    pair_width = keyvalue_weight.shape[2]
    flat_keyval = keyvalue_weight.reshape(model_width, 2 * pair_width)
    row_table, filled = slot_table(row_adapter_index, per_adapter_rows, owners)
    slot_list = row_table[owner_index]
    slot_valid = filled[owner_index]
    local_slot = row_adapter_index[slot_list] - owner_index * per_adapter_rows
    selector = (
        (local_slot[:, None] == jnp.arange(per_adapter_rows, dtype=jnp.int32)[None, :])
        & slot_valid[:, None]
    ).astype(jnp.float32)
    gathered = lax.all_gather(normed, "row", axis=0, tiled=True)
    base_query_output = jnp.dot(gathered, query_weight, preferred_element_type=jnp.float32)
    base_kv = jnp.dot(gathered, flat_keyval, preferred_element_type=jnp.float32)
    selected_down = jnp.take(gathered, slot_list, axis=0)
    down_projected = jnp.einsum(
        "mo,lto->mlt", selected_down, adapter_down_weight, preferred_element_type=jnp.float32
    )
    reduced = jnp.sum(down_projected * selector[:, :, None], axis=1)
    scattered = (
        jnp.zeros((row_total, 2 * reduced_rank_state), jnp.float32).at[slot_list].add(reduced)
    )
    low_vectors = lax.psum(scattered, "row")
    low_bf = low_vectors.astype(jnp.bfloat16)
    selected_query_up = jnp.take(adapter_query_up, row_adapter_index, axis=0)
    selected_value_up = jnp.take(adapter_value_up, row_adapter_index, axis=0)
    query_correction = jnp.einsum(
        "rk,rkc->rc",
        low_bf[:, :reduced_rank_state],
        selected_query_up,
        preferred_element_type=jnp.float32,
    )
    value_correction = jnp.einsum(
        "rk,rkc->rc",
        low_bf[:, reduced_rank_state:],
        selected_value_up,
        preferred_element_type=jnp.float32,
    )
    query_column_part = (base_query_output + adapter_scale * query_correction).astype(jnp.bfloat16)
    keyvalue_divided = base_kv.reshape(row_total, 2, pair_width)
    key_cols = keyvalue_divided[:, 0, :].astype(jnp.bfloat16)
    value_column_part = (keyvalue_divided[:, 1, :] + adapter_scale * value_correction).astype(
        jnp.bfloat16
    )
    pair_cols = jnp.stack([key_cols, value_column_part], axis=1)
    query_rows, pair_rows = (
        lax.all_to_all(
            query_column_part[:, None, :], "row", split_axis=0, concat_axis=2, tiled=True
        ),
        lax.all_to_all(pair_cols, "row", split_axis=0, concat_axis=2, tiled=True),
    )
    return attend(
        query_rows[:, 0, :],
        pair_rows[:, 0, :],
        pair_rows[:, 1, :],
        cached_rotated_keys,
        cached_value_rows,
    )


def solution(mesh):
    return jax.shard_map(
        shards,
        mesh=mesh,
        in_specs=(
            P(("grp", "row"), None),
            P(),
            P(None, "row"),
            P(None, None, "row"),
            P("row", None, None),
            P(None, None, "row"),
            P(None, None, "row"),
            P(("grp", "row"), None, None),
            P(("grp", "row"), None, None),
            P("grp"),
        ),
        out_specs=(P(("grp", "row"), None), P(("grp", "row"), None), P(("grp", "row"), None)),
        check_vma=False,
    )
```

profile of v0, /device:TPU:0, one launch (start us, length us, event | category | flops | bytes accessed | tf_op | source)
XLA Modules:
  0.0 195.0 jit_solution(14031582706016681155)
XLA Ops:
  7.2 1.3 fusion.31
  8.5 1.8 fusion.33
  10.3 3.8 %sort.17 = (s32[256]{0:T(256)}, s32[256]{0:T(256)S(1)}) sort(s32[256]{0:T(256)} %param.19, s32[256]{0:T(256)S(1)} %iota.44), dimensions={0}, to_apply=%region_2.3 | sort | flops 2048 | bytes 4096 | tf_op jit(solution)/shard_map/jit(argsort)/sort | solution.py:39
  14.2 0.7 and_select_fusion
  15.4 6.8 %gather_fusion = s32[1024]{0:T(1024)S(1)} fusion(s32[256]{0:T(256)S(1)} %get-tuple-element.4, s32[1024]{0:T(1024)S(1)} %broadcast_clamp_fusion), kind=kCustom, calls=%fused_computation | custom fusion | bytes 12288 | tf_op jit(solution)/shard_map/gather | solution.py:49
  22.4 0.8 gather_fusion.2
  23.2 2.2 %gather_fusion.4 = bf16[256,32,64]{2,1,0:T(8,128)(2,1)} fusion(bf16[64,32,64]{2,1,0:T(8,128)(2,1)S(1)} %copy-done.4, s32[1024]{0:T(1024)S(1)} %pad_clamp_fusion), kind=kCustom, calls=%fused_computation.4 | custom fusion | bytes 2098176 | tf_op jit(solution)/shard_map/jit(_take)/gather | solution.py:136
  25.5 8.6 %gather_fusion.3 = bf16[256,32,512]{2,1,0:T(8,128)(2,1)} fusion(bf16[64,32,512]{2,1,0:T(8,128)(2,1)S(1)} %copy-done, s32[1024]{0:T(1024)S(1)} %pad_clamp_fusion), kind=kCustom, calls=%fused_computation.3 | custom fusion | bytes 16778240 | tf_op jit(solution)/shard_map/jit(_take)/gather | solution.py:135
  34.2 29.9 %all-gather.2.cloned.1.call-done = bf16[256,8192]{1,0:T(8,128)(2,1)} async-done(((bf16[16,8192]{1,0:T(8,128)(2,1)}), bf16[256,8192]{1,0:T(8,128)(2,1)}) %all-gather.2.cloned.1.call-update) | async-done | bytes 4194320 | tf_op jit(solution)/shard_map/all_gather | solution.py:122
  64.1 4.4 %fusion.3 = f32[256,2,64]{0,2,1:T(8,128)S(1)} fusion(bf16[256,8192]{1,0:T(8,128)(2,1)} %all-gather.2.cloned.1.call-done, bf16[8192,2,64]{0,2,1:T(8,128)(2,1)} %param.13), kind=kOutput, calls=%fused_computation.9 | convolution fusion | flops 536870912 | bytes 6422528 | tf_op jit(solution)/shard_map/dot_general | solution.py:124
  68.5 4.9 %gather_fusion.1 = bf16[64,8192]{1,0:T(8,128)(2,1)S(1)} fusion(bf16[256,8192]{1,0:T(8,128)(2,1)} %all-gather.2.cloned.1.call-done, s32[1024]{0:T(1024)S(1)} %pad_clamp_fusion.1), kind=kCustom, calls=%fused_computation.1 | custom fusion | bytes 2097408 | tf_op jit(solution)/shard_map/jit(_take)/gather | solution.py:125
  73.4 4.3 %fusion.26 = f32[64,64]{1,0:T(8,128)S(1)} fusion(bf16[4,64,8192]{2,1,0:T(8,128)(2,1)} %param.14, bf16[64,8192]{1,0:T(8,128)(2,1)S(1)} %gather_fusion.1, pred[64]{0:T(512)(128)(4,1)S(1)} %get-tuple-element.5, f32[64,4]{0,1:T(4,128)S(1)} %fusion.48), kind=kOutput, calls=%fused_computation.32 | convolution fusion | flops 268988416 | bytes 5260352 | tf_op jit(solution)/shard_map/mo,lto->mlt/dot_general | solution.py:126
  77.7 1.0 scatter_custom_fusion
  78.8 60.0 %psum.7 = bf16[256,64]{1,0:T(8,128)(2,1)S(1)} all-reduce(f32[256,64]{1,0:T(8,128)S(1)} %scatter_custom_fusion), channel_id=1, replica_groups=mesh['grp'=2,'row'=16] {'row'}, use_global_device_ids=true, to_apply=%region_6.7 | all-reduce | flops 16384 | bytes 98304 | tf_op jit(solution)/shard_map/psum | solution.py:133
  138.8 2.3 %fusion.7 = f32[256,1,64]{2,1,0:T(1,128)S(1)} fusion(bf16[256,32,64]{2,1,0:T(8,128)(2,1)} %gather_fusion.4, pred[256]{0:T(512)(128)(4,1)S(1)} %compare_and_fusion, bf16[256,32,1]{1,0,2:T(8,128)(2,1)S(1)} %get-tuple-element.19), kind=kOutput, calls=%fused_computation.13 | convolution fusion | flops 1572864 | bytes 1130752 | tf_op jit(solution)/shard_map/rk,rkc->rc/dot_general | solution.py:143
  141.4 0.8 reshape.300
  142.2 3.7 %all-to-all-start.1 = ((bf16[16,2,1024]{2,1,0:T(2,128)(2,1)}), bf16[16,2,1024]{2,1,0:T(2,128)(2,1)S(1)}, u32[]{:S(2)}, u32[]{:S(2)}) async-start(bf16[16,2,1024]{2,1,0:T(2,128)(2,1)} %reshape.300), calls=%async_computation.1 | async-start | bytes 131072 | tf_op jit(solution)/shard_map/all_to_all | solution.py:160
  145.9 4.8 %fusion = f32[256,1,512]{2,1,0:T(1,128)S(1)} fusion(bf16[256,32,512]{2,1,0:T(8,128)(2,1)} %gather_fusion.3, pred[256]{0:T(512)(128)(4,1)S(1)} %compare_and_fusion, bf16[256,32,1]{1,0,2:T(8,128)(2,1)S(1)} %get-tuple-element.18), kind=kOutput, calls=%fused_computation.6 | convolution fusion | flops 12582912 | bytes 8929536 | tf_op jit(solution)/shard_map/rk,rkc->rc/dot_general | solution.py:137
  150.7 5.7 %fusion.24 = bf16[256,1,512]{2,0,1:T(8,128)(2,1)S(1)} fusion(bf16[256,8192]{1,0:T(8,128)(2,1)S(1)} %copy-done.2, bf16[8192,512]{1,0:T(8,128)(2,1)} %param.12, f32[256,1,512]{2,1,0:T(1,128)S(1)} %fusion), kind=kOutput, calls=%fused_computation.29 | convolution fusion | flops 2147876864 | bytes 13369344 | tf_op jit(solution)/shard_map/dot_general | solution.py:123
  156.9 0.8 reduce.3
  157.7 0.9 reshape.302
  158.6 5.8 %all-to-all-start = ((bf16[16,2,4096]{2,1,0:T(2,128)(2,1)}), bf16[16,2,4096]{2,1,0:T(2,128)(2,1)S(1)}, u32[]{:S(2)}, u32[]{:S(2)}) async-start(bf16[16,2,4096]{2,1,0:T(2,128)(2,1)} %reshape.302), calls=%async_computation | async-start | bytes 524288 | tf_op jit(solution)/shard_map/all_to_all | solution.py:157
  164.8 0.6 slice_bitcast_fusion.3
  166.3 8.1 %all-to-all-done = bf16[16,2,4096]{2,1,0:T(2,128)(2,1)S(1)} async-done(((bf16[16,2,4096]{2,1,0:T(2,128)(2,1)}), bf16[16,2,4096]{2,1,0:T(2,128)(2,1)S(1)}, u32[]{:S(2)}, u32[]{:S(2)}) %all-to-all-start) | async-done | bytes 262176 | tf_op jit(solution)/shard_map/all_to_all | solution.py:157
  175.7 0.8 copy-done.5
  176.5 1.0 fusion.14
  177.5 1.7 copy.92
  179.2 2.7 %fusion.59 = (f32[16,8,8]{0,2,1:T(8,128)S(1)}, f32[16,8,8,48]{0,2,3,1:T(8,128)}) fusion(f32[16,8,8,48]{0,2,3,1:T(8,128)} %copy.92), kind=kLoop, calls=%fused_computation.111 | loop fusion | flops 97280 | bytes 397312 | tf_op jit(solution)/shard_map/reduce_max | solution.py:78
  182.2 1.9 fusion.25
  184.5 0.8 copy.99
  185.4 1.9 fusion.21
  187.3 0.9 copy.138
  (65 shorter events, 4.9 us)
Async XLA Ops:
  7.2 18.3 %copy-start = (bf16[64,32,512]{2,1,0:T(8,128)(2,1)S(1)}, bf16[64,32,512]{2,1,0:T(8,128)(2,1)}, u32[]{:S(2)}) copy-start(bf16[64,32,512]{2,1,0:T(8,128)(2,1)} %param.15) | copy-start | bytes 6291460
  7.2 56.9 %all-gather.2.cloned.1.call-start = ((), (), s32[]{:S(2)}) async-start(), calls=%async_computation.2 | async-start | bytes 4456448 | tf_op jit(solution)/shard_map/all_gather | solution.py:122
  15.4 7.0 %copy-start.1 = (s32[256]{0:T(256)S(1)}, s32[256]{0:T(256)}, u32[]{:S(2)}) copy-start(s32[256]{0:T(256)} %param.19) | copy-start | bytes 3076
  15.4 7.8 %copy-start.4 = (bf16[64,32,64]{2,1,0:T(8,128)(2,1)S(1)}, bf16[64,32,64]{2,1,0:T(8,128)(2,1)}, u32[]{:S(2)}) copy-start(bf16[64,32,64]{2,1,0:T(8,128)(2,1)} %param.16) | copy-start | bytes 786436
  142.2 16.4 %all-to-all-start.1 = ((bf16[16,2,1024]{2,1,0:T(2,128)(2,1)}), bf16[16,2,1024]{2,1,0:T(2,128)(2,1)S(1)}, u32[]{:S(2)}, u32[]{:S(2)}) async-start(bf16[16,2,1024]{2,1,0:T(2,128)(2,1)} %reshape.300), calls=%async_computation.1 | async-start | bytes 131072 | tf_op jit(solution)/shard_map/all_to_all | solution.py:160
  145.8 4.8 %copy-start.2 = (bf16[256,8192]{1,0:T(8,128)(2,1)S(1)}, bf16[256,8192]{1,0:T(8,128)(2,1)}, u32[]{:S(2)}) copy-start(bf16[256,8192]{1,0:T(8,128)(2,1)} %all-gather.2.cloned.1.call-done) | copy-start | bytes 12582916
  158.6 15.8 %all-to-all-start = ((bf16[16,2,4096]{2,1,0:T(2,128)(2,1)}), bf16[16,2,4096]{2,1,0:T(2,128)(2,1)S(1)}, u32[]{:S(2)}, u32[]{:S(2)}) async-start(bf16[16,2,4096]{2,1,0:T(2,128)(2,1)} %reshape.302), calls=%async_computation | async-start | bytes 524288 | tf_op jit(solution)/shard_map/all_to_all | solution.py:157
  175.1 1.4 copy-start.5
  182.2 1.9 copy-start.3
Sparse Core Ops, SparseCore 0:
  10.7 53.2 all-gather.1
where the time goes:
time: 196 us; the launch traced here: 195 us
  blocking collectives  60 us (31%)
  waiting for transfers between devices  38 us (19%)
  local copies, waits for them, and re-layouts  32.2 us (16%)
  matrix products  24.8 us (13%)
  other arithmetic  16 us (8%)
  between operations  14.4 us (7%)
  starting transfers between devices  9.49 us (5%)
    psum x1, blocking collectives, shards(): low_vectors = lax.psum(scattered, 'row')  60 us
    all_gather x1, waiting for transfers between devices, shards(): gathered = lax.all_gather(normed, 'row', axis=0, tiled=True)  29.9 us
    gather x1, local copies, waits for them, and re-layouts, shards(): selected_query_up = jnp.take(adapter_query_up, row_adapter_index, axis=0)  8.61 us
    all_to_all x1, waiting for transfers between devices, shards(): lax.all_to_all(query_column_part[:, None, :], 'row', split_axis=0, concat...  8.12 us
    gather x2, local copies, waits for them, and re-layouts, slot_table(): sorted_rows[jnp.minimum(positions, row_total - 1)]  6.9 us
    all_to_all x1, starting transfers between devices, shards(): lax.all_to_all(query_column_part[:, None, :], 'row', split_axis=0, concat...  5.79 us
    dot_general x1, matrix products, shards(): jnp.dot(gathered, query_weight, preferred_element_type=jnp.float32)  5.71 us
    gather x1, local copies, waits for them, and re-layouts, shards(): selected_down = jnp.take(gathered, slot_list, axis=0)  4.88 us
  transfers between devices with their start and end apart: 3, of which 2 were waited for; matrix products, arithmetic and copies ran while one was open for 20% of the time, Pallas kernels for 0%

commit v1 on v0

v1 whole, which is shorter than its diff:
```python
import math

import jax
import jax.numpy as jnp
from jax import lax
from jax.experimental import pallas as pl
from jax.experimental.pallas import tpu as pltpu
from jax.sharding import PartitionSpec as P

HEAD_DIM = 128
CAPO = 64
LANES = 128
MESH = pl.DeviceIdType.MESH

eps_value = 1e-05
adapter_scale = 2.0
rope_base = 500000.0

K_PIECES = 4
CHUNK_CHIPS = 4


def rotation_table(position):
    half_width = HEAD_DIM // 2
    fraction = jnp.arange(half_width, dtype=jnp.float32) / half_width
    angles = position * jnp.exp(-fraction * math.log(rope_base))
    cosine = jnp.cos(angles)
    sine_part = jnp.sin(angles)
    return jnp.stack(
        [jnp.concatenate([cosine, cosine]), jnp.concatenate([-sine_part, sine_part])]
    )


def row_codes(row_adapter_index, per_adapter_rows):
    owner = row_adapter_index // per_adapter_rows
    places = jnp.arange(owner.shape[0], dtype=jnp.int32)
    earlier = (owner[:, None] == owner[None, :]) & (places[None, :] < places[:, None])
    rank = jnp.sum(earlier.astype(jnp.int32), axis=1)
    code = row_adapter_index * CAPO + rank
    return jnp.broadcast_to(code[:, None], (owner.shape[0], LANES))


def kernel(
    n,
    adapters,
    own,
    tokens_ref,
    gain_ref,
    table_ref,
    code_ref,
    wq_hbm,
    down_hbm,
    wkv_hbm,
    uq_hbm,
    uv_hbm,
    keys_hbm,
    values_hbm,
    context_ref,
    new_keys_ref,
    new_values_ref,
    gathered,
    wq,
    side,
    uq,
    uv,
    keys,
    values,
    acc,
    acc_side,
    compact,
    low_slots,
    out_blocks,
    in_blocks,
    load_sem,
    ring_send,
    ring_recv,
    sib_send,
    sib_recv,
    low_send,
    low_recv,
    out_send,
    in_recv,
):
    group = lax.axis_index("grp")
    me = lax.axis_index("row")
    rows, width = tokens_ref.shape
    chips = n // 2
    far = chips // 2
    half = width // 2
    q_cols = wq.shape[1]
    k_cols = wkv_hbm.shape[0] // 2
    downs = down_hbm.shape[0]
    core = lax.rem(me, 2)
    chip = me // 2
    snake = chips == 8

    def to_position(c):
        if not snake:
            return c
        z, y = c // 2, lax.rem(c, 2)
        return z + y * (chips - 1 - 2 * z)

    def to_chip(p):
        if not snake:
            return p
        y = p // far
        return 2 * (p + y * (chips - 1 - 2 * p)) + y

    place = to_position(chip)

    def device_at(offset, other_core):
        c = to_chip(lax.rem(place + (offset + chips), chips))
        return 2 * c + (1 - core if other_core else core)

    neighbours = (device_at(1, False), device_at(-1, False))
    sibling = 2 * chip + 1 - core

    def slot_of(way, s):
        if s == 0:
            return 0
        if s == far:
            return chips - 1
        return 2 * s - 1 + way

    slot_offset = [0] * chips
    for s in range(1, far):
        slot_offset[slot_of(0, s)] = -s
        slot_offset[slot_of(1, s)] = s
    slot_offset[chips - 1] = far
    block_device = [
        device_at(slot_offset[b // 2], b % 2 == 1) for b in range(n)
    ]

    loads = [
        pltpu.make_async_copy(a, b, load_sem.at[i])
        for i, (a, b) in enumerate(
            [
                (wq_hbm, wq),
                (down_hbm, side.at[pl.ds(0, downs), :]),
                (wkv_hbm, side.at[pl.ds(downs, 2 * k_cols), :]),
                (uq_hbm, uq),
                (uv_hbm, uv),
                (keys_hbm, keys),
                (values_hbm, values),
            ]
        )
    ]
    for load in loads:
        load.start()

    barrier = pltpu.get_barrier_semaphore()

    @pl.loop(1, n)
    def _(d):
        pl.semaphore_signal(
            barrier, inc=1, device_id=(group, lax.rem(me + d, n)), device_id_type=MESH
        )

    tokens = tokens_ref[...].astype(jnp.float32)
    mean_square = jnp.sum(tokens * tokens, axis=1, keepdims=True) / width
    gathered[0:rows, :] = (tokens * lax.rsqrt(mean_square + eps_value) * gain_ref[...]).astype(
        jnp.bfloat16
    )
    compact[...] = jnp.zeros_like(compact)
    pl.semaphore_wait(barrier, n - 1)

    def reach(way, h):
        return far if way == h else far - 1

    def block(slot, other, h):
        start = (2 * slot + other) * rows
        return gathered.at[pl.ds(start, rows), pl.ds(h * half, half)]

    def ring(way, s, h):
        i = (way * far + s - 1) * 2 + h
        return pltpu.make_async_remote_copy(
            src_ref=block(slot_of(way, s - 1), 0, h),
            dst_ref=block(slot_of(way, s), 0, h),
            send_sem=ring_send.at[i],
            recv_sem=ring_recv.at[i],
            device_id=(group, neighbours[way]),
            device_id_type=MESH,
        )

    def across(way, s, h):
        i = (way * (far + 1) + s) * 2 + h
        return pltpu.make_async_remote_copy(
            src_ref=block(slot_of(way, s), 0, h),
            dst_ref=block(slot_of(way, s), 1, h),
            send_sem=sib_send.at[i],
            recv_sem=sib_recv.at[i],
            device_id=(group, sibling),
            device_id_type=MESH,
        )

    ring_steps = [
        (way, s, h)
        for s in range(1, far + 1)
        for h in range(2)
        for way in range(2)
        if s <= reach(way, h)
    ]
    across_steps = [(0, 0, 0), (0, 0, 1)] + ring_steps

    for way, s, h in ring_steps:
        if s == 1:
            ring(way, s, h).start()
    across(0, 0, 0).start()
    across(0, 0, 1).start()

    chunk_rows = CHUNK_CHIPS * 2 * rows
    chunks = chips // CHUNK_CHIPS
    depth = width // K_PIECES
    arrived = set()

    def wait_across(chunk):
        for step in across_steps:
            if step not in arrived and slot_of(*step[:2]) // CHUNK_CHIPS <= chunk:
                arrived.add(step)
                across(*step).wait_recv()

    def add_to(total, at, piece, value):
        if piece == 0:
            total[at, :] = value
        else:
            total[at, :] += value

    def side_piece(chunk, piece):
        at = pl.ds(chunk * chunk_rows, chunk_rows)
        span = pl.ds(piece * depth, depth)
        product = lax.dot_general(
            gathered[at, span],
            side[:, span],
            (((1,), (1,)), ((), ())),
            preferred_element_type=jnp.float32,
        )
        add_to(acc_side, at, piece, product)

    def query_piece(chunk, piece):
        at = pl.ds(chunk * chunk_rows, chunk_rows)
        span = pl.ds(piece * depth, depth)
        product = jnp.dot(gathered[at, span], wq[span, :], preferred_element_type=jnp.float32)
        add_to(acc, at, piece, product)

    shape = (chunk_rows, LANES)
    lane = lax.broadcasted_iota(jnp.int32, shape, 1)
    own_bits = own.bit_length() - 1

    def chunk_codes(chunk):
        first = chunk * CHUNK_CHIPS * 2
        code = jnp.concatenate(
            [
                code_ref[pl.ds(pl.multiple_of(block_device[b] * rows, rows), rows), :]
                for b in range(first, first + CHUNK_CHIPS * 2)
            ],
            axis=0,
        )
        adapter = code >> 6
        return adapter, adapter >> own_bits, code & (CAPO - 1)

    def pack_low(chunk):
        adapter, owner, rank = chunk_codes(chunk)
        at = pl.ds(chunk * chunk_rows, chunk_rows)
        low = jnp.zeros(shape, jnp.float32)
        for t in range(own // 2):
            local = me * own + 2 * t + (lane >> 6)
            low += jnp.where(adapter == local, acc_side[at, t * LANES : (t + 1) * LANES], 0.0)
        low = low + pltpu.roll(low, 64, 1)
        chosen = jnp.where((rank == lane) & (owner == me), 1.0, 0.0).astype(jnp.bfloat16)
        compact[...] += lax.dot_general(
            chosen,
            low.astype(jnp.bfloat16),
            (((0,), (0,)), ((), ())),
            preferred_element_type=jnp.float32,
        )

    todo = []

    def fill():
        if todo:
            todo.pop(0)()

    def queue(chunk):
        def first():
            wait_across(chunk)
            if chunk == 0:
                loads[0].wait()
                loads[1].wait()
                loads[2].wait()

        def make(piece):
            def run():
                if piece == 0:
                    first()
                side_piece(chunk, piece)
                query_piece(chunk, piece)
                if piece == K_PIECES - 1:
                    pack_low(chunk)

            return run

        todo.extend(make(piece) for piece in range(K_PIECES))

    queued = 0
    for s in range(1, far + 1):
        for h in range(2):
            for way in range(2):
                if s > reach(way, h):
                    continue
                ring(way, s, h).wait_recv()
                if s + 1 <= reach(way, h):
                    ring(way, s + 1, h).start()
                across(way, s, h).start()
            fill()
        while queued < chunks - 1 and (queued + 1) * CHUNK_CHIPS <= 2 * s + 1:
            queue(queued)
            queued += 1
    while todo:
        fill()
    last = chunks - 1
    wait_across(last)
    for piece in range(K_PIECES):
        side_piece(last, piece)
    pack_low(last)

    lane32 = lax.broadcasted_iota(jnp.int32, (CAPO // 2, LANES), 1)
    low_slots[me] = jnp.where(
        lane32 < 64, compact[0 : CAPO // 2, :], compact[CAPO // 2 : CAPO, :]
    ).astype(jnp.bfloat16)

    def low_copy(d):
        return pltpu.make_async_remote_copy(
            src_ref=low_slots.at[me],
            dst_ref=low_slots.at[me],
            send_sem=low_send.at[d],
            recv_sem=low_recv.at[me],
            device_id=(group, lax.rem(me + d, n)),
            device_id_type=MESH,
        )

    def low_arrival(d):
        source = lax.rem(me + d, n)
        return pltpu.make_async_remote_copy(
            src_ref=low_slots.at[source],
            dst_ref=low_slots.at[source],
            send_sem=low_send.at[d],
            recv_sem=low_recv.at[source],
            device_id=(group, source),
            device_id_type=MESH,
        )

    @pl.loop(1, n)
    def _(d):
        low_copy(d).start()

    for piece in range(K_PIECES):
        query_piece(last, piece)

    @pl.loop(1, n)
    def _(d):
        low_arrival(d).wait_recv()

    loads[3].wait()
    loads[4].wait()

    def out_copy(b):
        return pltpu.make_async_remote_copy(
            src_ref=out_blocks.at[b],
            dst_ref=in_blocks.at[me],
            send_sem=out_send.at[b],
            recv_sem=in_recv.at[me],
            device_id=(group, block_device[b]),
            device_id_type=MESH,
        )

    def in_arrival(b):
        source = block_device[b]
        return pltpu.make_async_remote_copy(
            src_ref=out_blocks.at[b],
            dst_ref=in_blocks.at[source],
            send_sem=out_send.at[b],
            recv_sem=in_recv.at[source],
            device_id=(group, source),
            device_id_type=MESH,
        )

    all_low = low_slots[...].reshape(n * (CAPO // 2), LANES)
    for chunk in range(chunks):
        at = pl.ds(chunk * chunk_rows, chunk_rows)
        adapter, owner, rank = chunk_codes(chunk)
        target = owner * (CAPO // 2) + (rank & (CAPO // 2 - 1))
        expand = jnp.concatenate(
            [
                jnp.where(target == lane + t * LANES, 1.0, 0.0).astype(jnp.bfloat16)
                for t in range(n * (CAPO // 2) // LANES)
            ],
            axis=1,
        )
        low = jnp.dot(expand, all_low, preferred_element_type=jnp.float32)
        low = jnp.where((rank >> 5) == (lane >> 6), low, 0.0) * adapter_scale
        low = low + pltpu.roll(low, 64, 1)
        turned = pltpu.roll(low, 32, 1)
        even = ((lane >> 5) & 1) == 0
        low_q = jnp.where(even, low, turned)
        low_v = jnp.where(even, turned, low)
        spread_q, spread_v = [], []
        for t in range(adapters * 32 // LANES):
            hit = adapter == 4 * t + (lane >> 5)
            spread_q.append(jnp.where(hit, low_q, 0.0).astype(jnp.bfloat16))
            spread_v.append(jnp.where(hit, low_v, 0.0).astype(jnp.bfloat16))
        query = acc[at, :] + jnp.dot(
            jnp.concatenate(spread_q, axis=1), uq[...], preferred_element_type=jnp.float32
        )
        shift = jnp.dot(
            jnp.concatenate(spread_v, axis=1), uv[...], preferred_element_type=jnp.float32
        )
        pair = acc_side[at, downs : downs + 2 * k_cols]
        pair = jnp.concatenate([pair[:, :k_cols], pair[:, k_cols:] + shift], axis=1)
        query = query.astype(jnp.bfloat16)
        pair = pair.astype(jnp.bfloat16)
        for i in range(CHUNK_CHIPS * 2):
            b = chunk * CHUNK_CHIPS * 2 + i
            out_blocks[b, :, 0:q_cols] = query[i * rows : (i + 1) * rows, :]
            out_blocks[b, :, q_cols : q_cols + 2 * k_cols] = pair[i * rows : (i + 1) * rows, :]
            if b > 0:
                out_copy(b).start()
        if chunk == 0:
            in_blocks[me] = out_blocks[0]

    loads[5].wait()
    loads[6].wait()
    for b in range(1, n):
        in_arrival(b).wait_recv()

    heads = n * q_cols // HEAD_DIM
    kv_heads = n * k_cols // HEAD_DIM
    per_kv = heads // kv_heads
    sharers = n // kv_heads
    cached = keys.shape[0]
    prefix = cached // rows
    cosine = table_ref[0:1, :]
    sine = table_ref[1:2, :]

    def rotate(vectors):
        vectors = vectors.astype(jnp.float32)
        return (vectors * cosine + pltpu.roll(vectors, HEAD_DIM // 2, 1) * sine).astype(
            jnp.bfloat16
        )

    stacked = per_kv * rows
    row_of = lax.broadcasted_iota(jnp.int32, (stacked, cached), 0) & (rows - 1)
    column = lax.broadcasted_iota(jnp.int32, (stacked, cached), 1)
    same_row = (column >= row_of * prefix) & (column < (row_of + 1) * prefix)
    scale = HEAD_DIM ** (-0.5)
    for k in range(kv_heads):
        span = pl.ds(k * HEAD_DIM, HEAD_DIM)
        pieces = [in_blocks[k * sharers + i] for i in range(sharers)]
        query = jnp.concatenate(
            [
                piece[:, j * HEAD_DIM : (j + 1) * HEAD_DIM]
                for piece in pieces
                for j in range(q_cols // HEAD_DIM)
            ],
            axis=0,
        )
        key_new = jnp.concatenate([p[:, q_cols : q_cols + k_cols] for p in pieces], axis=1)
        value_new = jnp.concatenate(
            [p[:, q_cols + k_cols : q_cols + 2 * k_cols] for p in pieces], axis=1
        )
        query = rotate(query)
        key_new = rotate(key_new)
        new_keys_ref[:, span] = key_new
        new_values_ref[:, span] = value_new
        old = lax.dot_general(
            query, keys[:, span], (((1,), (1,)), ((), ())), preferred_element_type=jnp.float32
        )
        old = jnp.where(same_row, old * scale, -1e30)
        key_all = jnp.concatenate([key_new.astype(jnp.float32)] * per_kv, axis=0)
        value_all = jnp.concatenate([value_new.astype(jnp.float32)] * per_kv, axis=0)
        fresh = jnp.sum(query.astype(jnp.float32) * key_all, axis=1, keepdims=True) * scale
        peak = jnp.maximum(jnp.max(old, axis=1, keepdims=True), fresh)
        expo = jnp.exp(old - peak)
        expo_new = jnp.exp(fresh - peak)
        share = 1.0 / (jnp.sum(expo, axis=1, keepdims=True) + expo_new)
        weights = (expo * share).astype(jnp.bfloat16)
        weight_new = (expo_new * share).astype(jnp.bfloat16).astype(jnp.float32)
        mixed = jnp.dot(weights, values[:, span], preferred_element_type=jnp.float32)
        mixed = (mixed + weight_new * value_all).astype(jnp.bfloat16)
        for j in range(per_kv):
            at = (k * per_kv + j) * HEAD_DIM
            context_ref[:, at : at + HEAD_DIM] = mixed[j * rows : (j + 1) * rows, :]

    for step in ring_steps:
        ring(*step).wait_send()
    for step in across_steps:
        across(*step).wait_send()

    @pl.loop(1, n)
    def _(d):
        low_copy(d).wait_send()

    for b in range(1, n):
        out_copy(b).wait_send()


def shards(
    tokens,
    attention_norm_gain,
    query_weight,
    keyvalue_weight,
    adapter_down_weight,
    adapter_query_up,
    adapter_value_up,
    cached_rotated_keys,
    cached_value_rows,
    row_adapter_index,
):
    n = lax.axis_size("row")
    rows, width = tokens.shape
    total = row_adapter_index.shape[0]
    own, ranks, _ = adapter_down_weight.shape
    adapters, rank, q_cols = adapter_query_up.shape
    k_cols = keyvalue_weight.shape[2]
    prefix, kv_width = cached_rotated_keys.shape[1:]
    table = rotation_table(float(prefix))
    code = row_codes(row_adapter_index, own)
    wkv = jnp.transpose(keyvalue_weight, (1, 2, 0)).reshape(2 * k_cols, width)
    down = adapter_down_weight.reshape(own * ranks, width)
    uq = adapter_query_up.reshape(adapters * rank, q_cols)
    uv = adapter_value_up.reshape(adapters * rank, k_cols)
    keys = cached_rotated_keys.reshape(rows * prefix, kv_width)
    values = cached_value_rows.reshape(rows * prefix, kv_width)
    side_rows = own * ranks + 2 * k_cols
    hbm = [query_weight, down, wkv, uq, uv, keys, values]
    far = n // 4
    bf16, f32 = jnp.bfloat16, jnp.float32
    dma = pltpu.SemaphoreType.DMA

    def body(*refs):
        kernel(n, adapters, own, *refs)

    vmem = pl.BlockSpec(memory_space=pltpu.VMEM)
    return pl.pallas_call(
        body,
        out_shape=(
            jax.ShapeDtypeStruct((rows, n * q_cols), bf16),
            jax.ShapeDtypeStruct((rows, n * k_cols), bf16),
            jax.ShapeDtypeStruct((rows, n * k_cols), bf16),
        ),
        in_specs=[vmem] * 4 + [pl.BlockSpec(memory_space=pl.ANY)] * len(hbm),
        out_specs=(vmem, vmem, vmem),
        scratch_shapes=[pltpu.VMEM((total, width), bf16)]
        + [pltpu.VMEM(query_weight.shape, bf16), pltpu.VMEM((side_rows, width), bf16)]
        + [pltpu.VMEM(a.shape, bf16) for a in hbm[3:]]
        + [
            pltpu.VMEM((total, q_cols), f32),
            pltpu.VMEM((total, side_rows), f32),
            pltpu.VMEM((LANES, LANES), f32),
            pltpu.VMEM((n, CAPO // 2, LANES), bf16),
            pltpu.VMEM((n, rows, q_cols + 2 * k_cols), bf16),
            pltpu.VMEM((n, rows, q_cols + 2 * k_cols), bf16),
            dma((len(hbm),)),
            dma((4 * far,)),
            dma((4 * far,)),
            dma((4 * (far + 1),)),
            dma((4 * (far + 1),)),
            dma((n,)),
            dma((n,)),
            dma((n,)),
            dma((n,)),
        ],
        compiler_params=pltpu.CompilerParams(
            collective_id=0, has_side_effects=True, vmem_limit_bytes=56 * 1024 * 1024
        ),
    )(tokens, attention_norm_gain.reshape(1, width), table, code, *hbm)


def solution(mesh):
    return jax.shard_map(
        shards,
        mesh=mesh,
        in_specs=(
            P(("grp", "row"), None),
            P(),
            P(None, "row"),
            P(None, None, "row"),
            P("row", None, None),
            P(None, None, "row"),
            P(None, None, "row"),
            P(("grp", "row"), None, None),
            P(("grp", "row"), None, None),
            P("grp"),
        ),
        out_specs=(P(("grp", "row"), None), P(("grp", "row"), None), P(("grp", "row"), None)),
        check_vma=False,
    )
```

time: 196 us -> 64.4 us (0.33)
  blocking collectives: 60 us -> 0 us
  Pallas kernels: 0 us -> 55.8 us
  waiting for transfers between devices: 38 us -> 0 us
  local copies, waits for them, and re-layouts: 32.2 us -> 5.17 us
  matrix products: 24.8 us -> 0 us
  between operations: 14.4 us -> 0.65 us
  other arithmetic: 16 us -> 2.39 us
  starting transfers between devices: 9.49 us -> 0 us
    psum x1 -> x0, blocking collectives: 60 us -> none  [shards(): low_vectors = lax.psum(scattered, 'row')]
    pallas_call x0 -> x1, Pallas kernels: none -> 55.8 us  [shards(): pl.pallas_call(body, out_shape=(jax.ShapeDtypeStruct((rows, n * q_cols),...]
    all_gather x1 -> x0, waiting for transfers between devices: 29.9 us -> none  [shards(): gathered = lax.all_gather(normed, 'row', axis=0, tiled=True)]
    dot_general x8 -> x0, matrix products: 24.8 us -> none  [the longest x1 5.71 us: shards(): jnp.dot(gathered, query_weight, preferred_element_type=jnp.float32)]
    gather x6 -> x0, local copies, waits for them, and re-layouts: 23.4 us -> none  [the longest x1 8.61 us: shards(): selected_query_up = jnp.take(adapter_query_up, row_adapter_index, axis=0)]
    all_to_all x2 -> x0, starting transfers between devices: 9.45 us -> none  [the longest x1 5.79 us: shards(): lax.all_to_all(query_column_part[:, None, :], 'row', split_axis=0, concat...]
    all_to_all x2 -> x0, waiting for transfers between devices: 8.12 us -> none  [the longest x1 8.12 us: shards(): lax.all_to_all(query_column_part[:, None, :], 'row', split_axis=0, concat...]
    sort x1 -> x0, other arithmetic: 3.84 us -> none  [slot_table(): sorted_rows = jnp.argsort(row_adapter_index, stable=True)]
  transfers between devices with their start and end apart: 3 -> 0, of which waited for: 2 -> 0; matrix products, arithmetic and copies ran while one was open for 20% -> 0% of each run, Pallas kernels for 0% -> 0%
where the time goes in v1:
time: 64.4 us; the launch traced here: 64 us
  Pallas kernels  55.8 us (87%)
  local copies, waits for them, and re-layouts  5.17 us (8%)
  other arithmetic  2.39 us (4%)
  between operations  0.65 us (1%)
    pallas_call x1, Pallas kernels, shards(): pl.pallas_call(body, out_shape=(jax.ShapeDtypeStruct((rows, n * q_cols),...  55.8 us
    unnamed x3, local copies, waits for them, and re-layouts  4.42 us

profile of v1, /device:TPU:0, one launch (start us, length us, event | category | flops | bytes accessed | tf_op | source)
XLA Modules:
  0.0 64.0 jit_solution(3216476518750335860)
XLA Ops:
  0.6 0.1 fusion.2
  0.7 0.1 maximum_bitcast_fusion
  0.8 0.7 %and_select_fusion = s32[256]{0:T(256)S(1)} fusion(s32[256]{0:T(256)} %param.19), kind=kLoop, calls=%fused_computation.3 | loop fusion | flops 3840 | bytes 2048 | tf_op jit(solution)/shard_map/jit(floor_divide)/jit(_where)/select_n | solution.py:35
  1.5 0.2 convert_reduce_fusion
  1.6 0.7 %multiply_add_fusion = s32[256]{0:T(256)S(1)} fusion(s32[256]{0:T(256)S(1)} %convert_reduce_fusion, s32[256]{0:T(256)} %param.19), kind=kLoop, calls=%fused_computation.8 | loop fusion | flops 512 | bytes 3072 | tf_op jit(solution)/shard_map/add | solution.py:39
  2.3 0.1 fusion.1
  2.4 0.1 maximum_bitcast_fusion.1
  2.5 0.6 pad_maximum_fusion.refs_2_
  3.0 0.8 %broadcast_in_dim.2.refs_3_ = s32[256,128]{1,0:T(8,128)} broadcast(s32[256]{0:T(256)S(1)} %multiply_add_fusion), dimensions={0} | broadcast | bytes 132096 | tf_op jit(solution)/shard_map/broadcast_in_dim | solution.py:40
  3.8 55.8 %shard_map.121 = (bf16[16,8192]{1,0:T(8,128)(2,1)}, bf16[16,1024]{1,0:T(8,128)(2,1)}, bf16[16,1024]{1,0:T(8,128)(2,1)}) custom-call(bf16[16,8192]{1,0:T(8,128)(2,1)} %refs_0_.1, f32[1,8192]{1,0:T(1,128)} %bitcast.19, f32[2,128]{1,0:T(2,128)} %pad_maximum_fusion.refs_2_, s32[256,128]{1,0:T(8,128)} %broadcast_in_dim.2.refs_3_, bf16[8192,512]{1,0:T(8,128)(2,1)} %refs_4_.1, ...), custom_call_target="tpu_custom_call" | custom-call | tf_op jit(solution)/shard_map/pallas_call | solution.py:543
  59.6 1.7 %copy.16 = bf16[16,8192]{1,0:T(8,128)(2,1)} copy(bf16[16,8192]{1,0:T(8,128)(2,1)} %get-tuple-element.8) | data formatting | bytes 524288
  61.3 1.4 %copy.17 = bf16[16,1024]{1,0:T(8,128)(2,1)} copy(bf16[16,1024]{1,0:T(8,128)(2,1)} %get-tuple-element.9) | data formatting | bytes 65536
  62.7 1.4 %copy.18 = bf16[16,1024]{1,0:T(8,128)(2,1)} copy(bf16[16,1024]{1,0:T(8,128)(2,1)} %get-tuple-element.10) | data formatting | bytes 65536

commit v2 on v1

--- a/solution.py
+++ b/solution.py
@@ -2,6 +2,7 @@
 
 import jax
 import jax.numpy as jnp
+import numpy as np
 from jax import lax
 from jax.experimental import pallas as pl
 from jax.experimental.pallas import tpu as pltpu
@@ -17,27 +18,39 @@
 rope_base = 500000.0
 
 K_PIECES = 4
+PARTS = 4
 CHUNK_CHIPS = 4
 
 
 def rotation_table(position):
     half_width = HEAD_DIM // 2
-    fraction = jnp.arange(half_width, dtype=jnp.float32) / half_width
-    angles = position * jnp.exp(-fraction * math.log(rope_base))
-    cosine = jnp.cos(angles)
-    sine_part = jnp.sin(angles)
-    return jnp.stack(
-        [jnp.concatenate([cosine, cosine]), jnp.concatenate([-sine_part, sine_part])]
-    )
-
-
-def row_codes(row_adapter_index, per_adapter_rows):
-    owner = row_adapter_index // per_adapter_rows
-    places = jnp.arange(owner.shape[0], dtype=jnp.int32)
-    earlier = (owner[:, None] == owner[None, :]) & (places[None, :] < places[:, None])
-    rank = jnp.sum(earlier.astype(jnp.int32), axis=1)
-    code = row_adapter_index * CAPO + rank
-    return jnp.broadcast_to(code[:, None], (owner.shape[0], LANES))
+    fraction = np.arange(half_width, dtype=np.float32) / np.float32(half_width)
+    angles = np.float32(position) * np.exp(-fraction * np.float32(math.log(rope_base)))
+    cosine = np.cos(angles)
+    sine_part = np.sin(angles)
+    rows = [np.concatenate([cosine, cosine]), np.concatenate([-sine_part, sine_part])]
+    return jnp.asarray(np.stack(rows).astype(np.float32))
+
+
+def write_codes(index_ref, code_ref, own_bits):
+    square = (LANES, LANES)
+    lane = lax.broadcasted_iota(jnp.int32, square, 1)
+    row = lax.broadcasted_iota(jnp.int32, square, 0)
+    groups = index_ref.shape[0]
+    along = [
+        jnp.broadcast_to(index_ref[g : g + 1, :].astype(jnp.float32), square) for g in range(groups)
+    ]
+    for g in range(groups):
+        adapter = along[g].T.astype(jnp.int32)
+        owner = adapter >> own_bits
+        count = jnp.zeros(square, jnp.float32)
+        for other in range(g + 1):
+            same = (along[other].astype(jnp.int32) >> own_bits) == owner
+            if other == g:
+                same = same & (lane < row)
+            count += jnp.where(same, 1.0, 0.0)
+        rank = jnp.sum(count, axis=1, keepdims=True).astype(jnp.int32)
+        code_ref[g * LANES : (g + 1) * LANES, :] = adapter * CAPO + rank
 
 
 def kernel(
@@ -47,7 +60,7 @@
     tokens_ref,
     gain_ref,
     table_ref,
-    code_ref,
+    index_ref,
     wq_hbm,
     down_hbm,
     wkv_hbm,
@@ -58,6 +71,7 @@
     context_ref,
     new_keys_ref,
     new_values_ref,
+    code_ref,
     gathered,
     wq,
     side,
@@ -86,7 +100,7 @@
     rows, width = tokens_ref.shape
     chips = n // 2
     far = chips // 2
-    half = width // 2
+    part = width // PARTS
     q_cols = wq.shape[1]
     k_cols = wkv_hbm.shape[0] // 2
     downs = down_hbm.shape[0]
@@ -165,14 +179,14 @@
     pl.semaphore_wait(barrier, n - 1)
 
     def reach(way, h):
-        return far if way == h else far - 1
+        return far if way == h // (PARTS // 2) else far - 1
 
     def block(slot, other, h):
         start = (2 * slot + other) * rows
-        return gathered.at[pl.ds(start, rows), pl.ds(h * half, half)]
+        return gathered.at[pl.ds(start, rows), pl.ds(h * part, part)]
 
     def ring(way, s, h):
-        i = (way * far + s - 1) * 2 + h
+        i = (way * far + s - 1) * PARTS + h
         return pltpu.make_async_remote_copy(
             src_ref=block(slot_of(way, s - 1), 0, h),
             dst_ref=block(slot_of(way, s), 0, h),
@@ -183,7 +197,7 @@
         )
 
     def across(way, s, h):
-        i = (way * (far + 1) + s) * 2 + h
+        i = (way * (far + 1) + s) * PARTS + h
         return pltpu.make_async_remote_copy(
             src_ref=block(slot_of(way, s), 0, h),
             dst_ref=block(slot_of(way, s), 1, h),
@@ -196,18 +210,20 @@
     ring_steps = [
         (way, s, h)
         for s in range(1, far + 1)
-        for h in range(2)
+        for h in range(PARTS)
         for way in range(2)
         if s <= reach(way, h)
     ]
-    across_steps = [(0, 0, 0), (0, 0, 1)] + ring_steps
+    across_steps = [(0, 0, h) for h in range(PARTS)] + ring_steps
 
     for way, s, h in ring_steps:
         if s == 1:
             ring(way, s, h).start()
-    across(0, 0, 0).start()
-    across(0, 0, 1).start()
-
+    for h in range(PARTS):
+        across(0, 0, h).start()
+
+    own_bits = own.bit_length() - 1
+    write_codes(index_ref, code_ref, own_bits)
     chunk_rows = CHUNK_CHIPS * 2 * rows
     chunks = chips // CHUNK_CHIPS
     depth = width // K_PIECES
@@ -244,7 +260,6 @@
 
     shape = (chunk_rows, LANES)
     lane = lax.broadcasted_iota(jnp.int32, shape, 1)
-    own_bits = own.bit_length() - 1
 
     def chunk_codes(chunk):
         first = chunk * CHUNK_CHIPS * 2
@@ -303,7 +318,7 @@
 
     queued = 0
     for s in range(1, far + 1):
-        for h in range(2):
+        for h in range(PARTS):
             for way in range(2):
                 if s > reach(way, h):
                     continue
@@ -429,9 +444,6 @@
 
     loads[5].wait()
     loads[6].wait()
-    for b in range(1, n):
-        in_arrival(b).wait_recv()
-
     heads = n * q_cols // HEAD_DIM
     kv_heads = n * k_cols // HEAD_DIM
     per_kv = heads // kv_heads
@@ -452,8 +464,21 @@
     column = lax.broadcasted_iota(jnp.int32, (stacked, cached), 1)
     same_row = (column >= row_of * prefix) & (column < (row_of + 1) * prefix)
     scale = HEAD_DIM ** (-0.5)
-    for k in range(kv_heads):
-        span = pl.ds(k * HEAD_DIM, HEAD_DIM)
+    by_chip = sharers == 2
+    if not by_chip:
+        for b in range(1, n):
+            in_arrival(b).wait_recv()
+    order = range(chips)
+    for turn in range(kv_heads):
+        if by_chip:
+            slot = order[turn]
+            k = block_device[2 * slot] // 2
+            for b in (2 * slot, 2 * slot + 1):
+                if b > 0:
+                    in_arrival(b).wait_recv()
+        else:
+            k = turn
+        span = pl.ds(pl.multiple_of(k * HEAD_DIM, HEAD_DIM), HEAD_DIM)
         pieces = [in_blocks[k * sharers + i] for i in range(sharers)]
         query = jnp.concatenate(
             [
@@ -487,8 +512,8 @@
         mixed = jnp.dot(weights, values[:, span], preferred_element_type=jnp.float32)
         mixed = (mixed + weight_new * value_all).astype(jnp.bfloat16)
         for j in range(per_kv):
-            at = (k * per_kv + j) * HEAD_DIM
-            context_ref[:, at : at + HEAD_DIM] = mixed[j * rows : (j + 1) * rows, :]
+            at = pl.multiple_of((k * per_kv + j) * HEAD_DIM, HEAD_DIM)
+            context_ref[:, pl.ds(at, HEAD_DIM)] = mixed[j * rows : (j + 1) * rows, :]
 
     for step in ring_steps:
         ring(*step).wait_send()
@@ -501,6 +526,12 @@
 
     for b in range(1, n):
         out_copy(b).wait_send()
+
+
+def hand_over(a, b, c, a_out, b_out, c_out):
+    a_out[...] = a[...]
+    b_out[...] = b[...]
+    c_out[...] = c[...]
 
 
 def shards(
@@ -523,7 +554,7 @@
     k_cols = keyvalue_weight.shape[2]
     prefix, kv_width = cached_rotated_keys.shape[1:]
     table = rotation_table(float(prefix))
-    code = row_codes(row_adapter_index, own)
+    index = row_adapter_index.reshape(total // LANES, LANES)
     wkv = jnp.transpose(keyvalue_weight, (1, 2, 0)).reshape(2 * k_cols, width)
     down = adapter_down_weight.reshape(own * ranks, width)
     uq = adapter_query_up.reshape(adapters * rank, q_cols)
@@ -540,7 +571,7 @@
         kernel(n, adapters, own, *refs)
 
     vmem = pl.BlockSpec(memory_space=pltpu.VMEM)
-    return pl.pallas_call(
+    results = pl.pallas_call(
         body,
         out_shape=(
             jax.ShapeDtypeStruct((rows, n * q_cols), bf16),
@@ -549,7 +580,7 @@
         ),
         in_specs=[vmem] * 4 + [pl.BlockSpec(memory_space=pl.ANY)] * len(hbm),
         out_specs=(vmem, vmem, vmem),
-        scratch_shapes=[pltpu.VMEM((total, width), bf16)]
+        scratch_shapes=[pltpu.VMEM((total, LANES), jnp.int32), pltpu.VMEM((total, width), bf16)]
         + [pltpu.VMEM(query_weight.shape, bf16), pltpu.VMEM((side_rows, width), bf16)]
         + [pltpu.VMEM(a.shape, bf16) for a in hbm[3:]]
         + [
@@ -560,10 +591,10 @@
             pltpu.VMEM((n, rows, q_cols + 2 * k_cols), bf16),
             pltpu.VMEM((n, rows, q_cols + 2 * k_cols), bf16),
             dma((len(hbm),)),
-            dma((4 * far,)),
-            dma((4 * far,)),
-            dma((4 * (far + 1),)),
-            dma((4 * (far + 1),)),
+            dma((2 * PARTS * far,)),
+            dma((2 * PARTS * far,)),
+            dma((2 * PARTS * (far + 1),)),
+            dma((2 * PARTS * (far + 1),)),
             dma((n,)),
             dma((n,)),
             dma((n,)),
@@ -572,7 +603,13 @@
         compiler_params=pltpu.CompilerParams(
             collective_id=0, has_side_effects=True, vmem_limit_bytes=56 * 1024 * 1024
         ),
-    )(tokens, attention_norm_gain.reshape(1, width), table, code, *hbm)
+    )(tokens, attention_norm_gain.reshape(1, width), table, index, *hbm)
+    return pl.pallas_call(
+        hand_over,
+        out_shape=tuple(jax.ShapeDtypeStruct(a.shape, a.dtype) for a in results),
+        in_specs=[vmem] * 3,
+        out_specs=(vmem,) * 3,
+    )(*results)
 
 
 def solution(mesh):

time: 64.4 us -> 55.5 us (0.86); the launches traced: 64 us -> 54.4 us
  local copies, waits for them, and re-layouts: 5.17 us -> 0 us
  other arithmetic: 2.39 us -> 0 us
  Pallas kernels: 55.8 us -> 53.7 us
    unnamed x3 -> x0, local copies, waits for them, and re-layouts: 4.42 us -> none
    pallas_call x1, Pallas kernels: 55.8 us -> 52 us  [shards(): pl.pallas_call(body, out_shape=(jax.ShapeDtypeStruct((rows, n * q_cols),...]
    pallas_call x0 -> x1, Pallas kernels: none -> 1.7 us  [shards(): pl.pallas_call(hand_over, out_shape=tuple((jax.ShapeDtypeStruct(a.shape,...]
    broadcast_in_dim x1 -> x0, local copies, waits for them, and re-layouts: 0.75 us -> none  [row_codes(): return jnp.broadcast_to(code[:, None], (owner.shape[0], LANES))]
    another operation x3 -> x0, other arithmetic: 0.73 us -> none  [rotation_table(): jnp.stack([jnp.concatenate([cosine, cosine]), jnp.concatenate([-sine_part...]
    select_n x1 -> x0, other arithmetic: 0.69 us -> none  [row_codes(): owner = row_adapter_index // per_adapter_rows]
    add x1 -> x0, other arithmetic: 0.69 us -> none  [row_codes(): code = row_adapter_index * CAPO + rank]
where the time goes in v2:
time: 55.5 us; the launch traced here: 54.4 us
  Pallas kernels  53.7 us (97%)
  between operations  0.64 us (1%)
    pallas_call x1, Pallas kernels, shards(): pl.pallas_call(body, out_shape=(jax.ShapeDtypeStruct((rows, n * q_cols),...  52 us
    pallas_call x1, Pallas kernels, shards(): pl.pallas_call(hand_over, out_shape=tuple((jax.ShapeDtypeStruct(a.shape,...  1.7 us

profile of v2, /device:TPU:0, one launch (start us, length us, event | category | flops | bytes accessed | tf_op | source)
XLA Modules:
  0.0 54.4 jit_solution(16843652119441656370)
XLA Ops:
  0.6 52.0 %shard_map.130 = (bf16[16,8192]{1,0:T(8,128)(2,1)}, bf16[16,1024]{1,0:T(8,128)(2,1)}, bf16[16,1024]{1,0:T(8,128)(2,1)}) custom-call(bf16[16,8192]{1,0:T(8,128)(2,1)} %refs_0_.1, f32[1,8192]{1,0:T(1,128)} %bitcast.16, f32[2,128]{1,0:T(2,128)} %constant.2.clone.refs_2_, s32[2,128]{1,0:T(2,128)} %bitcast.17, bf16[8192,512]{1,0:T(8,128)(2,1)} %refs_4_.1, ...), custom_call_target="tpu_custom_call" | custom-call | tf_op jit(solution)/shard_map/pallas_call | solution.py:574
  52.7 1.7 %shard_map.131 = (bf16[16,8192]{1,0:T(8,128)(2,1)}, bf16[16,1024]{1,0:T(8,128)(2,1)}, bf16[16,1024]{1,0:T(8,128)(2,1)}) custom-call(bf16[16,8192]{1,0:T(8,128)(2,1)} %get-tuple-element.6.a, bf16[16,1024]{1,0:T(8,128)(2,1)} %get-tuple-element.7.b, bf16[16,1024]{1,0:T(8,128)(2,1)} %get-tuple-element.8.c), custom_call_target="tpu_custom_call" | custom-call | tf_op jit(solution)/shard_map/pallas_call | solution.py:607
